TPU v7x, 32 devices: a whole 2x2x4 slice. The times are simulated.
32 devices in a mesh: grp: 2 (over y), row: 4 (over x, core), col: 4 (over z).
Axes of the slice: x: 2, y: 2, z: 4, core: 2. Of those that a mesh axis runs over, the one named last changes fastest.
Arguments:
- gen_coords: bfloat16 [3, 192, 24576], P(None, None, ('grp', 'row', 'col')), parts along dimension 2, may hold values from -30 to 30
- ref_coords: bfloat16 [3, 192, 24576], P(None, None, ('grp', 'row', 'col')), parts along dimension 2, may hold values from -30 to 30
- threshold: float32 [1], replicated, may hold values from 0.75 to 2
Outputs:
- gen_best: float32 [24576], P(('grp', 'row', 'col')), parts along dimension 0
- ref_best: float32 [24576], P(('grp', 'row', 'col')), parts along dimension 0
- ref_cover: float32 [24576], P(('grp', 'row', 'col')), parts along dimension 0
There are 2 independent parts, one for each index of `grp`. A program takes and returns all parts, laid end to end along the dimension named above; an argument that names none is the same for every part. Nothing has to cross between parts.
All inputs are finite; a program needn't handle non-finite values.
Results may differ from a plain program's by a relative error of at most 0.0003.
Values may be sent and summed in bfloat16 or wider, within the bound.
A program may use at most 64 MiB of HBM per device.

v0:
```python
import jax
import jax.numpy as jnp
from jax import lax
from jax.sharding import PartitionSpec as P

ATOMS = 192
FRAMES = 768
POLAR = 8
STEPS = 2


soft_width = 0.25
floor_term = 0.01


def shifted(block, axis, distance):
    devices = range(lax.axis_size(axis))
    route = [((i - distance) % len(devices), i) for i in devices]
    return lax.ppermute(block, axis, route)


def centered(coords):
    points = coords.astype(jnp.float32)
    middle = jnp.mean(points, axis=1, keepdims=True)
    return points - middle


def squares(frames_c):
    return jnp.sum(frames_c * frames_c, axis=(0, 1))


def newton_trace(entries):
    squared = entries[0] * entries[0]
    for entry in entries[1:]:
        squared = squared + entry * entry
    inverse = lax.rsqrt(squared + 1.0)
    factor = [entry * inverse for entry in entries]
    for sweep in range(POLAR):
        gram = [
            [
                factor[source] * factor[target]
                + factor[3 + source] * factor[3 + target]
                + factor[6 + source] * factor[6 + target]
                for target in range(3)
            ]
            for source in range(3)
        ]
        factor = [
            1.5 * factor[3 * source + target]
            - 0.5
            * (
                factor[3 * source] * gram[0][target]
                + factor[3 * source + 1] * gram[1][target]
                + factor[3 * source + 2] * gram[2][target]
            )
            for source in range(3)
            for target in range(3)
        ]
    result = factor[0] * entries[0]
    for position in range(1, 9):
        result = result + factor[position] * entries[position]
    return result


def tile_stats(gen_raw, ref_raw, threshold):
    gen_c = centered(gen_raw)
    ref_c = centered(ref_raw)
    gen_sq = squares(gen_c)
    ref_sq = squares(ref_c)
    frames = gen_c.shape[2]
    block_width = min(128, frames)
    block_count = frames // block_width

    def visit(running, block_index):
        ref_low, ref_hits = running
        piece = lax.dynamic_slice_in_dim(gen_c, block_index * block_width, block_width, 2)
        piece_sq = lax.dynamic_slice_in_dim(gen_sq, block_index * block_width, block_width, 0)
        covariance = jnp.einsum("aif,bie->afbe", piece, ref_c, precision=lax.Precision.HIGHEST)
        entries = [covariance[source, :, target, :] for source in range(3) for target in range(3)]
        align = newton_trace(entries)
        rmsd = jnp.sqrt((piece_sq[:, None] + ref_sq[None, :] - 2.0 * align) / ATOMS + floor_term)
        weights = jax.nn.sigmoid((threshold - rmsd) / soft_width)
        return (
            (jnp.minimum(ref_low, jnp.min(rmsd, axis=0)), ref_hits + jnp.sum(weights, axis=0)),
            jnp.min(rmsd, axis=1),
        )

    start = (jnp.full((frames,), jnp.inf, jnp.float32), jnp.zeros((frames,), jnp.float32))
    (ref_low, ref_hits), gen_low = lax.scan(visit, start, jnp.arange(block_count, dtype=jnp.int32))
    return (gen_low.reshape(frames), ref_low, ref_hits)


def on_device(gen_coords, ref_coords, threshold):
    limit = threshold[0]
    ref_now = ref_coords
    row_index = lax.axis_index("row")
    row_count = lax.axis_size("row")
    gen_now = gen_coords
    for bit_index in range((row_count - 1).bit_length()):
        arrived = shifted(gen_now, "col", 1 << bit_index)
        gen_now = jnp.where((row_index >> bit_index) % 2 == 1, arrived, gen_now)
    gen_run = None
    ref_run = None
    ref_total = None
    for step_index in range(STEPS):
        gen_low, ref_low, ref_hits = tile_stats(gen_now, ref_now, limit)
        if step_index == 0:
            gen_run, ref_run, ref_total = (gen_low, ref_low, ref_hits)
        else:
            gen_run = jnp.minimum(gen_run, gen_low)
            ref_run = jnp.minimum(ref_run, ref_low)
            ref_total = ref_total + ref_hits
        if step_index + 1 < STEPS:
            gen_run = shifted(gen_run, "col", 1)
            ref_run, ref_total = shifted((ref_run, ref_total), "row", 1)
            ref_now = shifted(ref_now, "row", 1)
            gen_now = shifted(gen_now, "col", 1)
    back_amount = row_index + STEPS - 1
    for bit_index in range((row_count + STEPS - 2).bit_length()):
        arrived = shifted(gen_run, "col", -(1 << bit_index))
        gen_run = jnp.where((back_amount >> bit_index) % 2 == 1, arrived, gen_run)
    ref_run, ref_total = shifted((ref_run, ref_total), "row", 1 - STEPS)
    ref_cover = ref_total / (STEPS * FRAMES)
    return (gen_run, ref_run, ref_cover)


def solution(mesh):
    return jax.shard_map(
        on_device,
        mesh=mesh,
        in_specs=(P(None, None, ("grp", "row", "col")), P(None, None, ("grp", "row", "col")), P()),
        out_specs=(P(("grp", "row", "col")), P(("grp", "row", "col")), P(("grp", "row", "col"))),
        check_vma=False,
    )
```

profile of v0, /device:TPU:0, one launch (start us, length us, event | category | flops | bytes accessed | tf_op | source)
XLA Modules:
  0.0 347.4 jit_solution(15939731698507616404)
XLA Ops:
  0.6 3.1 collective-permute-start
  3.7 1.3 convert_reduce_fusion.2
  5.1 20.5 %collective-permute-done = bf16[3,192,768]{2,1,0:T(8,128)(2,1)S(1)} collective-permute-done((bf16[3,192,768]{2,1,0:T(8,128)(2,1)}, bf16[3,192,768]{2,1,0:T(8,128)(2,1)S(1)}, u32[]{:S(2)}, u32[]{:S(2)}) %collective-permute-start) | collective-permute-done | bytes 884768 | tf_op jit(solution)/shard_map/ppermute | solution.py:19
  25.6 1.3 broadcast_select_fusion
  28.9 1.4 convert_subtract_fusion
  30.3 35.0 %collective-permute-done.1 = bf16[3,192,768]{2,1,0:T(8,128)(2,1)S(1)} collective-permute-done((bf16[3,192,768]{2,1,0:T(8,128)(2,1)S(1)}, bf16[3,192,768]{2,1,0:T(8,128)(2,1)S(1)}, u32[]{:S(2)}, u32[]{:S(2)}) %collective-permute-start.1) | collective-permute-done | bytes 884768 | tf_op jit(solution)/shard_map/ppermute | solution.py:19
  65.3 1.2 convert_reduce_fusion.3
  66.5 3.2 convert_subtract_fusion.3
  70.8 132.4 %while.30 = (s32[]{:T(128)}, f32[768]{0:T(1024)}, f32[768]{0:T(1024)}, f32[6,128]{1,0:T(8,128)}, s32[6]{0:T(128)}, /*index=5*/f32[768]{0:T(1024)}, f32[768]{0:T(...) while((s32[]{:T(128)}, f32[768]{0:T(1024)}, ...), condition=%wide.region_8.9_spmd.clone, body=%wide.region_4.8_spmd.clone.sunk | while | flops 2124252544 | bytes 9173217 | solution.py:89
  70.8 1.2 dynamic_slice.40
  72.6 4.3 %fusion.32 = f32[3,128,3,768]{3,1,2,0:T(8,128)S(1)} fusion(f32[3,192,768]{2,1,0:T(8,128)S(1)} %get-tuple-element.421, f32[3,192,768]{2,1,0:T(8,128)} %get-tuple-element.420, s32[]{:T(128)S(6)} %select_n.96), kind=kOutput, calls=%fused_computation.clone.1 | convolution fusion | flops 2038431744 | bytes 5603332 | tf_op jit(solution)/shard_map/while/body/eval_jaxpr/aif,bie->afbe/dot_general | solution.py:78
  77.6 12.8 %fusion.33 = (f32[128]{0:T(128)}, f32[768]{0:T(1024)S(1)}, f32[768]{0:T(1024)S(1)}) fusion(f32[]{:T(128)} %get-tuple-element.422, f32[3,128,3,768]{3,1,2,0:T(8,128)S(1)} %fusion.32, f32[768]{0:T(1024)S(1)} %get-tuple-element.419, f32[128]{0:T(128)S(1)} %dynamic_slice.41), kind=kLoop, calls=%fused_computation.77.clone.1 | loop fusion | flops 85817728 | bytes 3549188 | tf_op jit(solution)/shard_map/while/body/eval_jaxpr/reduce_min | solution.py:85
  91.0 1.3 dynamic_update_slice.11
  94.1 4.3 %fusion.32 = f32[3,128,3,768]{3,1,2,0:T(8,128)S(1)} fusion(f32[3,192,768]{2,1,0:T(8,128)S(1)} %get-tuple-element.421, f32[3,192,768]{2,1,0:T(8,128)} %get-tuple-element.420, s32[]{:T(128)S(6)} %select_n.96), kind=kOutput, calls=%fused_computation.clone.1 | convolution fusion | flops 2038431744 | bytes 5603332 | tf_op jit(solution)/shard_map/while/body/eval_jaxpr/aif,bie->afbe/dot_general | solution.py:78
  99.1 12.8 %fusion.33 = (f32[128]{0:T(128)}, f32[768]{0:T(1024)S(1)}, f32[768]{0:T(1024)S(1)}) fusion(f32[]{:T(128)} %get-tuple-element.422, f32[3,128,3,768]{3,1,2,0:T(8,128)S(1)} %fusion.32, f32[768]{0:T(1024)S(1)} %get-tuple-element.419, f32[128]{0:T(128)S(1)} %dynamic_slice.41), kind=kLoop, calls=%fused_computation.77.clone.1 | loop fusion | flops 85817728 | bytes 3549188 | tf_op jit(solution)/shard_map/while/body/eval_jaxpr/reduce_min | solution.py:85
  111.9 1.3 select_add_fusion.4
  113.2 1.3 dynamic_update_slice.11
  116.3 4.3 %fusion.32 = f32[3,128,3,768]{3,1,2,0:T(8,128)S(1)} fusion(f32[3,192,768]{2,1,0:T(8,128)S(1)} %get-tuple-element.421, f32[3,192,768]{2,1,0:T(8,128)} %get-tuple-element.420, s32[]{:T(128)S(6)} %select_n.96), kind=kOutput, calls=%fused_computation.clone.1 | convolution fusion | flops 2038431744 | bytes 5603332 | tf_op jit(solution)/shard_map/while/body/eval_jaxpr/aif,bie->afbe/dot_general | solution.py:78
  121.3 12.8 %fusion.33 = (f32[128]{0:T(128)}, f32[768]{0:T(1024)S(1)}, f32[768]{0:T(1024)S(1)}) fusion(f32[]{:T(128)} %get-tuple-element.422, f32[3,128,3,768]{3,1,2,0:T(8,128)S(1)} %fusion.32, f32[768]{0:T(1024)S(1)} %get-tuple-element.419, f32[128]{0:T(128)S(1)} %dynamic_slice.41), kind=kLoop, calls=%fused_computation.77.clone.1 | loop fusion | flops 85817728 | bytes 3549188 | tf_op jit(solution)/shard_map/while/body/eval_jaxpr/reduce_min | solution.py:85
  134.1 1.3 select_add_fusion.4
  135.4 1.3 dynamic_update_slice.11
  138.5 4.3 %fusion.32 = f32[3,128,3,768]{3,1,2,0:T(8,128)S(1)} fusion(f32[3,192,768]{2,1,0:T(8,128)S(1)} %get-tuple-element.421, f32[3,192,768]{2,1,0:T(8,128)} %get-tuple-element.420, s32[]{:T(128)S(6)} %select_n.96), kind=kOutput, calls=%fused_computation.clone.1 | convolution fusion | flops 2038431744 | bytes 5603332 | tf_op jit(solution)/shard_map/while/body/eval_jaxpr/aif,bie->afbe/dot_general | solution.py:78
  143.5 12.8 %fusion.33 = (f32[128]{0:T(128)}, f32[768]{0:T(1024)S(1)}, f32[768]{0:T(1024)S(1)}) fusion(f32[]{:T(128)} %get-tuple-element.422, f32[3,128,3,768]{3,1,2,0:T(8,128)S(1)} %fusion.32, f32[768]{0:T(1024)S(1)} %get-tuple-element.419, f32[128]{0:T(128)S(1)} %dynamic_slice.41), kind=kLoop, calls=%fused_computation.77.clone.1 | loop fusion | flops 85817728 | bytes 3549188 | tf_op jit(solution)/shard_map/while/body/eval_jaxpr/reduce_min | solution.py:85
  156.3 1.3 select_add_fusion.4
  157.6 1.3 dynamic_update_slice.11
  160.6 4.3 %fusion.32 = f32[3,128,3,768]{3,1,2,0:T(8,128)S(1)} fusion(f32[3,192,768]{2,1,0:T(8,128)S(1)} %get-tuple-element.421, f32[3,192,768]{2,1,0:T(8,128)} %get-tuple-element.420, s32[]{:T(128)S(6)} %select_n.96), kind=kOutput, calls=%fused_computation.clone.1 | convolution fusion | flops 2038431744 | bytes 5603332 | tf_op jit(solution)/shard_map/while/body/eval_jaxpr/aif,bie->afbe/dot_general | solution.py:78
  165.6 12.8 %fusion.33 = (f32[128]{0:T(128)}, f32[768]{0:T(1024)S(1)}, f32[768]{0:T(1024)S(1)}) fusion(f32[]{:T(128)} %get-tuple-element.422, f32[3,128,3,768]{3,1,2,0:T(8,128)S(1)} %fusion.32, f32[768]{0:T(1024)S(1)} %get-tuple-element.419, f32[128]{0:T(128)S(1)} %dynamic_slice.41), kind=kLoop, calls=%fused_computation.77.clone.1 | loop fusion | flops 85817728 | bytes 3549188 | tf_op jit(solution)/shard_map/while/body/eval_jaxpr/reduce_min | solution.py:85
  178.4 1.3 select_add_fusion.4
  179.7 1.3 dynamic_update_slice.11
  182.8 4.3 %fusion.32 = f32[3,128,3,768]{3,1,2,0:T(8,128)S(1)} fusion(f32[3,192,768]{2,1,0:T(8,128)S(1)} %get-tuple-element.421, f32[3,192,768]{2,1,0:T(8,128)} %get-tuple-element.420, s32[]{:T(128)S(6)} %select_n.96), kind=kOutput, calls=%fused_computation.clone.1 | convolution fusion | flops 2038431744 | bytes 5603332 | tf_op jit(solution)/shard_map/while/body/eval_jaxpr/aif,bie->afbe/dot_general | solution.py:78
  187.8 12.8 %fusion.33 = (f32[128]{0:T(128)}, f32[768]{0:T(1024)S(1)}, f32[768]{0:T(1024)S(1)}) fusion(f32[]{:T(128)} %get-tuple-element.422, f32[3,128,3,768]{3,1,2,0:T(8,128)S(1)} %fusion.32, f32[768]{0:T(1024)S(1)} %get-tuple-element.419, f32[128]{0:T(128)S(1)} %dynamic_slice.41), kind=kLoop, calls=%fused_computation.77.clone.1 | loop fusion | flops 85817728 | bytes 3549188 | tf_op jit(solution)/shard_map/while/body/eval_jaxpr/reduce_min | solution.py:85
  200.6 1.3 select_add_fusion.4
  201.9 1.3 dynamic_update_slice.11
  203.3 1.3 convert_reduce_fusion.1
  204.6 2.0 convert_subtract_fusion.1
  207.7 125.7 %while.31 = (s32[]{:T(128)}, f32[768]{0:T(1024)S(1)}, f32[768]{0:T(1024)}, f32[6,128]{1,0:T(8,128)}, s32[6]{0:T(128)}, /*index=5*/f32[768]{0:T(1024)}, f32[768]{...) while((s32[]{:T(128)}, f32[768]{0:T(1024)S(1)}, ...), condition=%wide.region_17.18_spmd.clone, body=%wide.region_13.17_spmd.clone.sunk | while | flops 2124252544 | bytes 9173217 | solution.py:89
  209.4 3.3 fusion.36
  213.5 12.8 %fusion.37 = (f32[128]{0:T(128)}, f32[768]{0:T(1024)S(1)}, f32[768]{0:T(1024)S(1)}) fusion(f32[]{:T(128)} %get-tuple-element.464, f32[3,128,3,768]{3,1,2,0:T(8,128)S(1)} %fusion.36, f32[768]{0:T(1024)S(1)} %get-tuple-element.461, f32[128]{0:T(128)S(1)} %dynamic_slice.44), kind=kLoop, calls=%fused_computation.78.clone.1 | loop fusion | flops 85817728 | bytes 3549188 | tf_op jit(solution)/shard_map/while/body/eval_jaxpr/reduce_min | solution.py:85
  226.9 1.3 dynamic_update_slice.12
  229.8 3.3 fusion.36
  233.9 12.8 %fusion.37 = (f32[128]{0:T(128)}, f32[768]{0:T(1024)S(1)}, f32[768]{0:T(1024)S(1)}) fusion(f32[]{:T(128)} %get-tuple-element.464, f32[3,128,3,768]{3,1,2,0:T(8,128)S(1)} %fusion.36, f32[768]{0:T(1024)S(1)} %get-tuple-element.461, f32[128]{0:T(128)S(1)} %dynamic_slice.44), kind=kLoop, calls=%fused_computation.78.clone.1 | loop fusion | flops 85817728 | bytes 3549188 | tf_op jit(solution)/shard_map/while/body/eval_jaxpr/reduce_min | solution.py:85
  246.6 1.3 select_add_fusion.5
  247.9 1.3 dynamic_update_slice.12
  250.9 3.3 fusion.36
  254.9 12.8 %fusion.37 = (f32[128]{0:T(128)}, f32[768]{0:T(1024)S(1)}, f32[768]{0:T(1024)S(1)}) fusion(f32[]{:T(128)} %get-tuple-element.464, f32[3,128,3,768]{3,1,2,0:T(8,128)S(1)} %fusion.36, f32[768]{0:T(1024)S(1)} %get-tuple-element.461, f32[128]{0:T(128)S(1)} %dynamic_slice.44), kind=kLoop, calls=%fused_computation.78.clone.1 | loop fusion | flops 85817728 | bytes 3549188 | tf_op jit(solution)/shard_map/while/body/eval_jaxpr/reduce_min | solution.py:85
  267.7 1.3 select_add_fusion.5
  269.0 1.3 dynamic_update_slice.12
  271.9 3.3 fusion.36
  276.0 12.8 %fusion.37 = (f32[128]{0:T(128)}, f32[768]{0:T(1024)S(1)}, f32[768]{0:T(1024)S(1)}) fusion(f32[]{:T(128)} %get-tuple-element.464, f32[3,128,3,768]{3,1,2,0:T(8,128)S(1)} %fusion.36, f32[768]{0:T(1024)S(1)} %get-tuple-element.461, f32[128]{0:T(128)S(1)} %dynamic_slice.44), kind=kLoop, calls=%fused_computation.78.clone.1 | loop fusion | flops 85817728 | bytes 3549188 | tf_op jit(solution)/shard_map/while/body/eval_jaxpr/reduce_min | solution.py:85
  288.8 1.3 select_add_fusion.5
  290.0 1.3 dynamic_update_slice.12
  293.0 3.3 fusion.36
  297.1 12.8 %fusion.37 = (f32[128]{0:T(128)}, f32[768]{0:T(1024)S(1)}, f32[768]{0:T(1024)S(1)}) fusion(f32[]{:T(128)} %get-tuple-element.464, f32[3,128,3,768]{3,1,2,0:T(8,128)S(1)} %fusion.36, f32[768]{0:T(1024)S(1)} %get-tuple-element.461, f32[128]{0:T(128)S(1)} %dynamic_slice.44), kind=kLoop, calls=%fused_computation.78.clone.1 | loop fusion | flops 85817728 | bytes 3549188 | tf_op jit(solution)/shard_map/while/body/eval_jaxpr/reduce_min | solution.py:85
  309.8 1.3 select_add_fusion.5
  311.1 1.3 dynamic_update_slice.12
  314.1 3.3 fusion.36
  318.1 12.8 %fusion.37 = (f32[128]{0:T(128)}, f32[768]{0:T(1024)S(1)}, f32[768]{0:T(1024)S(1)}) fusion(f32[]{:T(128)} %get-tuple-element.464, f32[3,128,3,768]{3,1,2,0:T(8,128)S(1)} %fusion.36, f32[768]{0:T(1024)S(1)} %get-tuple-element.461, f32[128]{0:T(128)S(1)} %dynamic_slice.44), kind=kLoop, calls=%fused_computation.78.clone.1 | loop fusion | flops 85817728 | bytes 3549188 | tf_op jit(solution)/shard_map/while/body/eval_jaxpr/reduce_min | solution.py:85
  330.9 1.3 select_add_fusion.5
  332.2 1.3 dynamic_update_slice.12
  334.1 3.7 %collective-permute-start.5 = (f32[768]{0:T(1024)S(1)}, f32[768]{0:T(1024)S(1)}, u32[]{:S(2)}, u32[]{:S(2)}) collective-permute-start(f32[768]{0:T(1024)S(1)} %bitcast_minimum_fusion), channel_id=1, source_target_pairs={{1,0},{2,1},{3,2},{0,3},{5,4},{6,5},{7,6},{4,7},{9,8},{10,9},{11,1... | collective-permute-start | bytes 9224 | tf_op jit(solution)/shard_map/ppermute | solution.py:19
  337.8 1.6 collective-permute-start.10
  339.5 2.6 collective-permute-start.6
  342.7 1.6 collective-permute-start.11
  344.3 1.3 collective-permute-done.11
  (69 shorter events, 30.5 us)
Async XLA Ops:
  0.6 27.0 %copy-start = (bf16[3,192,768]{2,1,0:T(8,128)(2,1)S(1)}, bf16[3,192,768]{2,1,0:T(8,128)(2,1)}, u32[]{:S(2)}) copy-start(bf16[3,192,768]{2,1,0:T(8,128)(2,1)} %param.8) | copy-start | bytes 2654212
  0.6 25.0 %collective-permute-start = (bf16[3,192,768]{2,1,0:T(8,128)(2,1)}, bf16[3,192,768]{2,1,0:T(8,128)(2,1)S(1)}, u32[]{:S(2)}, u32[]{:S(2)}) collective-permute-start(bf16[3,192,768]{2,1,0:T(8,128)(2,1)} %param.7), channel_id=1, source_target_pairs={{3,0},{0,1},{1,2},{2,3},{7,4},{4,5},{5,6},{6,7},{11,8},{8,9},{9,10... | collective-permute-start | bytes 2654216 | tf_op jit(solution)/shard_map/ppermute | solution.py:19
  3.7 24.2 %collective-permute-start.4 = (bf16[3,192,768]{2,1,0:T(8,128)(2,1)}, bf16[3,192,768]{2,1,0:T(8,128)(2,1)S(1)}, u32[]{:S(2)}, u32[]{:S(2)}) collective-permute-start(bf16[3,192,768]{2,1,0:T(8,128)(2,1)} %param.8), channel_id=1, source_target_pairs={{12,0},{0,4},{4,8},{8,12},{13,1},{1,5},{5,9},{9,13},{14,2},{2,6},{... | collective-permute-start | bytes 2654216 | tf_op jit(solution)/shard_map/ppermute | solution.py:19
  26.9 38.4 %collective-permute-start.1 = (bf16[3,192,768]{2,1,0:T(8,128)(2,1)S(1)}, bf16[3,192,768]{2,1,0:T(8,128)(2,1)S(1)}, u32[]{:S(2)}, u32[]{:S(2)}) collective-permute-start(bf16[3,192,768]{2,1,0:T(8,128)(2,1)S(1)} %broadcast_select_fusion), channel_id=1, source_target_pairs={{2,0},{3,1},{0,2},{1,3},{6,4},{7,5},{4,6},{5,7},{10,8},{11,9},{8,1... | collective-permute-start | bytes 2654216 | tf_op jit(solution)/shard_map/ppermute | solution.py:19
  27.9 0.9 copy-start.1
  66.5 136.8 %collective-permute-start.3 = (bf16[3,192,768]{2,1,0:T(8,128)(2,1)}, bf16[3,192,768]{2,1,0:T(8,128)(2,1)}, u32[]{:S(2)}, u32[]{:S(2)}) collective-permute-start(bf16[3,192,768]{2,1,0:T(8,128)(2,1)} %get-tuple-element.230), channel_id=1, source_target_pairs={{3,0},{0,1},{1,2},{2,3},{7,4},{4,5},{5,6},{6,7},{11,8},{8,9},{9,10... | collective-permute-start | bytes 2654216 | tf_op jit(solution)/shard_map/ppermute | solution.py:19
  203.2 4.5 %copy-start.2 = (f32[768]{0:T(1024)S(1)}, f32[768]{0:T(1024)}, u32[]{:S(2)}) copy-start(f32[768]{0:T(1024)} %custom-call.2) | copy-start | bytes 9220
  203.2 130.2 %collective-permute-start.2 = (f32[768]{0:T(1024)}, f32[768]{0:T(1024)}, u32[]{:S(2)}, u32[]{:S(2)}) collective-permute-start(f32[768]{0:T(1024)} %bitcast.114), channel_id=1, source_target_pairs={{3,0},{0,1},{1,2},{2,3},{7,4},{4,5},{5,6},{6,7},{11,8},{8,9},{9,10... | collective-permute-start | bytes 9224 | tf_op jit(solution)/shard_map/ppermute | solution.py:19
  334.1 5.3 %collective-permute-start.5 = (f32[768]{0:T(1024)S(1)}, f32[768]{0:T(1024)S(1)}, u32[]{:S(2)}, u32[]{:S(2)}) collective-permute-start(f32[768]{0:T(1024)S(1)} %bitcast_minimum_fusion), channel_id=1, source_target_pairs={{1,0},{2,1},{3,2},{0,3},{5,4},{6,5},{7,6},{4,7},{9,8},{10,9},{11,1... | collective-permute-start | bytes 9224 | tf_op jit(solution)/shard_map/ppermute | solution.py:19
  337.8 4.2 %collective-permute-start.8 = (f32[768]{0:T(1024)}, f32[768]{0:T(1024)S(1)}, u32[]{:S(2)}, u32[]{:S(2)}) collective-permute-start(f32[768]{0:T(1024)} %get-tuple-element.113), channel_id=1, source_target_pairs={{12,0},{0,4},{4,8},{8,12},{13,1},{1,5},{5,9},{9,13},{14,2},{2,6},{... | collective-permute-start | bytes 9224 | tf_op jit(solution)/shard_map/ppermute | solution.py:19
  337.8 4.2 %collective-permute-start.10 = (f32[768]{0:T(1024)}, f32[768]{0:T(1024)S(1)}, u32[]{:S(2)}, u32[]{:S(2)}) collective-permute-start(f32[768]{0:T(1024)} %get-tuple-element.115), channel_id=1, source_target_pairs={{12,0},{0,4},{4,8},{8,12},{13,1},{1,5},{5,9},{9,13},{14,2},{2,6},{... | collective-permute-start | bytes 9224 | tf_op jit(solution)/shard_map/ppermute | solution.py:19
  339.5 4.9 %collective-permute-start.6 = (f32[768]{0:T(1024)S(1)}, f32[768]{0:T(1024)S(1)}, u32[]{:S(2)}, u32[]{:S(2)}) collective-permute-start(f32[768]{0:T(1024)S(1)} %broadcast_select_fusion.2), channel_id=1, source_target_pairs={{2,0},{3,1},{0,2},{1,3},{6,4},{7,5},{4,6},{5,7},{10,8},{11,9},{8,1... | collective-permute-start | bytes 9224 | tf_op jit(solution)/shard_map/ppermute | solution.py:19
  342.0 4.2 %collective-permute-start.9 = (f32[768]{0:T(1024)S(1)}, f32[768]{0:T(1024)S(1)}, u32[]{:S(2)}, u32[]{:S(2)}) collective-permute-start(f32[768]{0:T(1024)S(1)} %min.13), channel_id=1, source_target_pairs={{4,0},{8,4},{12,8},{0,12},{5,1},{9,5},{13,9},{1,13},{6,2},{10,6},{... | collective-permute-start | bytes 9224 | tf_op jit(solution)/shard_map/ppermute | solution.py:19
  342.7 2.9 collective-permute-start.11
  344.3 1.9 collective-permute-start.7
where the time goes:
time: 350 us; the launch traced here: 347 us
  other arithmetic  182 us (52%)
  waiting for transfers between devices  56.8 us (16%)
  matrix products  45.2 us (13%)
  local copies, waits for them, and re-layouts  41.9 us (12%)
  starting transfers between devices  13.5 us (4%)
  loops' own time  7.09 us (2%)
    reduce_min x12, other arithmetic, visit(): jnp.min(rmsd, axis=1)  153 us
    ppermute x12, waiting for transfers between devices, shifted(): return lax.ppermute(block, axis, route)  56.8 us
    dot_general x12, matrix products, visit(): jnp.einsum('aif,bie->afbe', piece, ref_c, precision=lax.Precision.HIGHEST)  45.2 us
    dynamic_update_slice x12, local copies, waits for them, and re-layouts, tile_stats(): lax.scan(visit, start, jnp.arange(block_count, dtype=jnp.int32))  15.3 us
    add x12, other arithmetic, visit(): ref_hits + jnp.sum(weights, axis=0)  14.1 us
    dynamic_slice x12, local copies, waits for them, and re-layouts, tile_stats(): lax.scan(visit, start, jnp.arange(block_count, dtype=jnp.int32))  13.9 us
    ppermute x12, starting transfers between devices, shifted(): return lax.ppermute(block, axis, route)  13.5 us
    dynamic_slice x12, local copies, waits for them, and re-layouts, visit(): lax.dynamic_slice_in_dim(gen_sq, block_index * block_width, block_width, 0)  9.06 us
  transfers between devices with their start and end apart: 12, of which 3 were waited for; matrix products, arithmetic and copies ran while one was open for 76% of the time, Pallas kernels for 0%

commit v1 on v0

v1 whole, which is shorter than its diff:
```python
import functools

import jax
import jax.numpy as jnp
from jax import lax
from jax.experimental import pallas as pl
from jax.experimental.pallas import tpu as pltpu
from jax.sharding import PartitionSpec as P

POLAR = 8
STEPS = 2
DEPTH = 256
LANES = 128

soft_width = 0.25
floor_term = 0.01

THIRD = (
    0.8660254163908417, 0.16666504306323746, -0.048077350345029135, 0.024392383831939313,
    -0.014289564826206913, 0.007664301754289227, -0.002922830501063345, 0.0005426077123047435,
)


def split3(x):
    one = x.astype(jnp.bfloat16).astype(jnp.float32)
    rest = x - one
    two = rest.astype(jnp.bfloat16).astype(jnp.float32)
    return (one, two, rest - two)


def align_of(h):
    h00, h01, h02, h10, h11, h12, h20, h21, h22 = h
    s00 = h00 * h00 + h10 * h10 + h20 * h20
    s11 = h01 * h01 + h11 * h11 + h21 * h21
    s22 = h02 * h02 + h12 * h12 + h22 * h22
    s01 = h00 * h01 + h10 * h11 + h20 * h21
    s02 = h00 * h02 + h10 * h12 + h20 * h22
    s12 = h01 * h02 + h11 * h12 + h21 * h22
    det = (
        h00 * (h11 * h22 - h12 * h21)
        - h01 * (h10 * h22 - h12 * h20)
        + h02 * (h10 * h21 - h11 * h20)
    )
    trace = s00 + s11 + s22
    minors = (s00 * s11 - s01 * s01) + (s00 * s22 - s02 * s02) + (s11 * s22 - s12 * s12)
    size = trace + 1.0
    inverse = lax.rsqrt(size)
    inv2 = inverse * inverse
    third = trace * inv2 * (1.0 / 3.0)
    c2 = minors * (inv2 * inv2)
    det_n = det * (inv2 * inverse)
    third2 = third * third
    p2 = jnp.maximum(third2 - c2 * (1.0 / 3.0), 1e-12)
    half = third * (third2 - 0.5 * c2) + 0.5 * (det_n * det_n)
    ip = lax.rsqrt(p2)
    p = p2 * ip
    ratio = half * (ip * ip * ip)
    r = jnp.minimum(jnp.abs(ratio), 1.0)
    c = THIRD[-1] * r + THIRD[-2]
    for k in THIRD[-3::-1]:
        c = c * r + k
    rest = jnp.maximum(1.0 - c * c, 1e-14)
    wide = (p * 0.8660254037844386) * (rest * lax.rsqrt(rest))
    signed = jnp.where(half < 0.0, -p, p)
    pc = signed * c
    base = third * 0.5 - 0.5 * pc
    roots = (third * 0.5 + pc, base + wide, base - wide)
    total = None
    for root in roots:
        root = jnp.maximum(root, 1e-20)
        start = root * lax.rsqrt(root)
        v = start * (1.5 - root)
        for _ in range(POLAR - 1):
            v = v * (1.5 - v * v)
        total = start * v if total is None else total + start * v
    return (size * inverse) * total


def kernel(atoms, frames, chunk, rows, thr_ref, gen_ref, ref_ref, gmin_ref, rmin_ref, rsum_ref,
           ref_t, gen_b, h, rnb, gnb, rmin, rsum, gmin):
    scale = 1.0 / atoms

    def load(source, columns):
        parts = []
        sq = None
        for a in range(3):
            x = source[a, :, columns].astype(jnp.float32)
            total = jnp.sum(x, axis=0, keepdims=True)
            d = x - total * scale
            q = jnp.sum(d * d, axis=0, keepdims=True)
            sq = q if sq is None else sq + q
            parts.append((x, total))
        return parts, sq * scale

    def rows_of(values, columns):
        zero = jnp.zeros((DEPTH - atoms - 16, columns), jnp.float32)
        pick = lax.broadcasted_iota(jnp.int32, (16, columns), 0)
        extra = jnp.zeros((16, columns), jnp.float32)
        for k, value in enumerate(values):
            extra = jnp.where(pick == k, value, extra)
        return extra, zero

    for start in range(0, frames, 256):
        columns = slice(start, start + 256)
        parts, sq = load(ref_ref, columns)
        rnb[columns, :] = jnp.broadcast_to(sq + floor_term, (LANES, 256)).T
        for a, (x, total) in enumerate(parts):
            s = split3(-total)
            extra, zero = rows_of([s[k % 3] for k in range(9)], 256)
            ref_t[a, columns, :] = jnp.concatenate([x, extra, zero], axis=0).T.astype(jnp.bfloat16)
    rmin[...] = jnp.full(rmin.shape, jnp.inf, jnp.float32)
    rsum[...] = jnp.zeros(rsum.shape, jnp.float32)
    limit = thr_ref[0] * (1.4426950408889634 / soft_width)

    for start in range(0, frames, chunk):
        columns = slice(start, start + chunk)
        parts, sq = load(gen_ref, columns)
        gnb[...] = jnp.broadcast_to(sq, (8, chunk))
        for a, (x, total) in enumerate(parts):
            m = split3(total * scale)
            extra, zero = rows_of([m[k // 3] for k in range(9)], chunk)
            gen_b[...] = jnp.concatenate([x, extra, zero], axis=0).astype(jnp.bfloat16)
            for b in range(3):
                h[3 * a + b] = jnp.dot(ref_t[b], gen_b[...], preferred_element_type=jnp.float32)
        gmin[...] = jnp.full(gmin.shape, jnp.inf, jnp.float32)

        def group(index, carry):
            at = pl.ds(pl.multiple_of(index * rows, rows), rows)
            align = align_of([h[k, at, :] for k in range(9)])
            rn = rnb[at, :]
            rn = jnp.concatenate([rn] * (chunk // LANES), axis=1)
            gn = jnp.concatenate([gnb[...]] * (rows // 8), axis=0)
            square = rn + gn - align * (4.0 * scale)
            rmsd = square * lax.rsqrt(square)
            power = jnp.minimum(rmsd * (1.4426950408889634 / soft_width) - limit, 120.0)
            weight = 1.0 / (1.0 + jnp.exp2(power))
            low, hits = rmsd[:, :LANES], weight[:, :LANES]
            for k in range(1, chunk // LANES):
                low = jnp.minimum(low, rmsd[:, k * LANES:(k + 1) * LANES])
                hits = hits + weight[:, k * LANES:(k + 1) * LANES]
            rmin[at, :] = jnp.minimum(rmin[at, :], low)
            rsum[at, :] = rsum[at, :] + hits
            best = rmsd[:8]
            for k in range(1, rows // 8):
                best = jnp.minimum(best, rmsd[8 * k:8 * k + 8])
            gmin[...] = jnp.minimum(gmin[...], best)
            return carry

        lax.fori_loop(0, frames // rows, group, 0)
        gmin_ref[:, columns] = jnp.min(gmin[...], axis=0, keepdims=True)

    rmin_ref[...] = jnp.min(rmin[...].T, axis=0, keepdims=True)
    rsum_ref[...] = jnp.sum(rsum[...].T, axis=0, keepdims=True)


def tile(gen, ref, threshold):
    _, atoms, frames = gen.shape
    chunk, rows = 256, 8
    row = jax.ShapeDtypeStruct((1, frames), jnp.float32)
    vmem = pl.BlockSpec(memory_space=pltpu.VMEM)
    out = pl.pallas_call(
        functools.partial(kernel, atoms, frames, chunk, rows),
        out_shape=(row, row, row),
        in_specs=[pl.BlockSpec(memory_space=pltpu.SMEM), vmem, vmem],
        out_specs=(vmem, vmem, vmem),
        scratch_shapes=[
            pltpu.VMEM((3, frames, DEPTH), jnp.bfloat16),
            pltpu.VMEM((DEPTH, chunk), jnp.bfloat16),
            pltpu.VMEM((9, frames, chunk), jnp.float32),
            pltpu.VMEM((frames, LANES), jnp.float32),
            pltpu.VMEM((8, chunk), jnp.float32),
            pltpu.VMEM((frames, LANES), jnp.float32),
            pltpu.VMEM((frames, LANES), jnp.float32),
            pltpu.VMEM((8, chunk), jnp.float32),
        ],
        compiler_params=pltpu.CompilerParams(vmem_limit_bytes=40 * 2**20),
        cost_estimate=pl.CostEstimate(flops=2 * 9 * atoms * frames * frames + 250 * frames * frames,
                                      bytes_accessed=12 * atoms * frames, transcendentals=0),
    )(threshold, gen, ref)
    return [x.reshape(frames) for x in out]


def on_device(gen_coords, ref_coords, threshold):
    height, width = lax.axis_size("row"), lax.axis_size("col")
    frames = gen_coords.shape[2]
    sources = []
    for step in range(STEPS):
        source = {}
        turn = step + step // width
        for i in range(height):
            for j in range(width):
                gen_row = (i + turn) % height
                source[i * width + j] = gen_row * width + (j - gen_row - step) % width
        sources.append(source)
    blocks = [
        lax.ppermute(gen_coords, ("row", "col"), [(s, d) for d, s in source.items()])
        for source in sources
    ]
    gen_best = ref_best = hits = None
    for source, block in zip(sources, blocks):
        g, r, w = tile(block, ref_coords, threshold)
        g = lax.ppermute(g, ("row", "col"), list(source.items()))
        gen_best = g if gen_best is None else jnp.minimum(gen_best, g)
        ref_best = r if ref_best is None else jnp.minimum(ref_best, r)
        hits = w if hits is None else hits + w
    return (gen_best, ref_best, hits / (STEPS * frames))


def solution(mesh):
    spread = ("grp", "row", "col")
    return jax.shard_map(
        on_device,
        mesh=mesh,
        in_specs=(P(None, None, spread), P(None, None, spread), P()),
        out_specs=(P(spread), P(spread), P(spread)),
        check_vma=False,
    )
```

time: 350 us -> 136 us (0.39)
  the two profiles are of different devices: /device:TPU:0 before, /device:TPU:1 now
where the time goes in v1:
time: 136 us
  Pallas kernels  80 us (59%)
  starting transfers between devices  35.9 us (26%)
  waiting for transfers between devices  16 us (12%)
    pallas_call x2, Pallas kernels, tile(): pl.pallas_call(functools.partial(kernel, atoms, frames, chunk, rows), out...  80 us
    ppermute x2, starting transfers between devices, on_device(): g = lax.ppermute(g, ('row', 'col'), list(source.items()))  30.4 us
    ppermute x2, waiting for transfers between devices, on_device(): lax.ppermute(gen_coords, ('row', 'col'), [(s, d) for d, s in source.items...  15.8 us
    ppermute x2, starting transfers between devices, on_device(): lax.ppermute(gen_coords, ('row', 'col'), [(s, d) for d, s in source.items...  5.52 us
  transfers between devices with their start and end apart: 4, of which 2 were waited for; matrix products, arithmetic and copies ran while one was open for 0% of the time, Pallas kernels for 59%

profile of v1, /device:TPU:1, one launch (start us, length us, event | category | flops | bytes accessed | tf_op | source)
XLA Modules:
  0.0 135.7 jit_solution(6660813093985323568)
XLA Ops:
  0.6 4.0 %collective-permute-start = (bf16[3,192,768]{2,1,0:T(8,128)(2,1)}, bf16[3,192,768]{2,1,0:T(8,128)(2,1)S(1)}, u32[]{:S(2)}, u32[]{:S(2)}) collective-permute-start(bf16[3,192,768]{2,1,0:T(8,128)(2,1)} %param.3), channel_id=1, source_target_pairs={{0,0},{1,1},{2,2},{3,3},{7,4},{4,5},{5,6},{6,7},{10,8},{11,9},{8,1... | collective-permute-start | bytes 2654216 | tf_op jit(solution)/shard_map/ppermute | solution.py:196
  4.7 1.5 %collective-permute-start.2 = (bf16[3,192,768]{2,1,0:T(8,128)(2,1)}, bf16[3,192,768]{2,1,0:T(8,128)(2,1)S(1)}, u32[]{:S(2)}, u32[]{:S(2)}) collective-permute-start(bf16[3,192,768]{2,1,0:T(8,128)(2,1)} %param.3), channel_id=1, source_target_pairs={{6,0},{7,1},{4,2},{5,3},{9,4},{10,5},{11,6},{8,7},{12,8},{13,9},{1... | collective-permute-start | bytes 2654216 | tf_op jit(solution)/shard_map/ppermute | solution.py:196
  6.8 15.8 %collective-permute-done.gen_ref = bf16[3,192,768]{2,1,0:T(8,128)(2,1)S(1)} collective-permute-done((bf16[3,192,768]{2,1,0:T(8,128)(2,1)}, bf16[3,192,768]{2,1,0:T(8,128)(2,1)S(1)}, u32[]{:S(2)}, u32[]{:S(2)}) %collective-permute-start) | collective-permute-done | bytes 884768 | tf_op jit(solution)/shard_map/ppermute | solution.py:196
  22.6 0.0 copy-start
  22.6 1.2 copy-done
  23.8 0.0 copy-start.1
  23.8 40.0 %shard_map.58 = (f32[1,768]{1,0:T(1,128)S(1)}, f32[1,768]{1,0:T(1,128)S(1)}, f32[1,768]{1,0:T(1,128)S(1)}) custom-call(f32[1]{0:T(128)S(6)} %copy.6.thr_ref, bf16[3,192,768]{2,1,0:T(8,128)(2,1)S(1)} %collective-permute-done.gen_ref, bf16[3,192,768]{2,1,0:T(8,128)(2,1)S(1)} %copy-done), custom_call_target="tpu_custom_call" | custom-call | flops 2185887744 | bytes 1769472 | tf_op jit(solution)/shard_map/pallas_call | solution.py:161
  63.8 5.7 %collective-permute-start.1 = (f32[768]{0:T(1024)S(1)}, f32[768]{0:T(1024)S(1)}, u32[]{:S(2)}, u32[]{:S(2)}) collective-permute-start(f32[768]{0:T(1024)S(1)} %reduce), channel_id=1, source_target_pairs={{0,0},{1,1},{2,2},{3,3},{4,7},{5,4},{6,5},{7,6},{8,10},{9,11},{10,... | collective-permute-start | bytes 9224 | tf_op jit(solution)/shard_map/ppermute | solution.py:202
  69.6 0.0 collective-permute-done.2.gen_ref
  69.6 0.0 copy-done.1
  69.6 40.0 %shard_map.59 = (f32[1,768]{1,0:T(1,128)S(1)}, f32[1,768]{1,0:T(1,128)S(1)}, f32[1,768]{1,0:T(1,128)S(1)}) custom-call(f32[1]{0:T(128)S(6)} %copy.6.thr_ref, bf16[3,192,768]{2,1,0:T(8,128)(2,1)S(1)} %collective-permute-done.2.gen_ref, bf16[3,192,768]{2,1,0:T(8,128)(2,1)S(1)} %copy-done.1), custom_call_target="tpu_custom_call" | custom-call | flops 2185887744 | bytes 1769472 | tf_op jit(solution)/shard_map/pallas_call | solution.py:161
  109.6 24.7 %collective-permute-start.3 = (f32[768]{0:T(1024)S(1)}, f32[768]{0:T(1024)S(1)}, u32[]{:S(2)}, u32[]{:S(2)}) collective-permute-start(f32[768]{0:T(1024)S(1)} %reduce.1), channel_id=1, source_target_pairs={{0,6},{1,7},{2,4},{3,5},{4,9},{5,10},{6,11},{7,8},{8,12},{9,13},{1... | collective-permute-start | bytes 9224 | tf_op jit(solution)/shard_map/ppermute | solution.py:202
  134.3 0.6 multiply_reduce_fusion
  134.9 0.0 collective-permute-done.1
  134.9 0.1 collective-permute-done.3
  135.1 0.6 min.9
  (2 shorter events, 0.0 us)
Async XLA Ops:
  0.6 22.0 %collective-permute-start = (bf16[3,192,768]{2,1,0:T(8,128)(2,1)}, bf16[3,192,768]{2,1,0:T(8,128)(2,1)S(1)}, u32[]{:S(2)}, u32[]{:S(2)}) collective-permute-start(bf16[3,192,768]{2,1,0:T(8,128)(2,1)} %param.3), channel_id=1, source_target_pairs={{0,0},{1,1},{2,2},{3,3},{7,4},{4,5},{5,6},{6,7},{10,8},{11,9},{8,1... | collective-permute-start | bytes 2654216 | tf_op jit(solution)/shard_map/ppermute | solution.py:196
  4.7 64.9 %collective-permute-start.2 = (bf16[3,192,768]{2,1,0:T(8,128)(2,1)}, bf16[3,192,768]{2,1,0:T(8,128)(2,1)S(1)}, u32[]{:S(2)}, u32[]{:S(2)}) collective-permute-start(bf16[3,192,768]{2,1,0:T(8,128)(2,1)} %param.3), channel_id=1, source_target_pairs={{6,0},{7,1},{4,2},{5,3},{9,4},{10,5},{11,6},{8,7},{12,8},{13,9},{1... | collective-permute-start | bytes 2654216 | tf_op jit(solution)/shard_map/ppermute | solution.py:196
  22.6 1.2 copy-start
  23.8 45.8 %copy-start.1 = (bf16[3,192,768]{2,1,0:T(8,128)(2,1)S(1)}, bf16[3,192,768]{2,1,0:T(8,128)(2,1)}, u32[]{:S(2)}) copy-start(bf16[3,192,768]{2,1,0:T(8,128)(2,1)} %ref_ref.3) | copy-start | bytes 2654212
  63.8 71.1 %collective-permute-start.1 = (f32[768]{0:T(1024)S(1)}, f32[768]{0:T(1024)S(1)}, u32[]{:S(2)}, u32[]{:S(2)}) collective-permute-start(f32[768]{0:T(1024)S(1)} %reduce), channel_id=1, source_target_pairs={{0,0},{1,1},{2,2},{3,3},{4,7},{5,4},{6,5},{7,6},{8,10},{9,11},{10,... | collective-permute-start | bytes 9224 | tf_op jit(solution)/shard_map/ppermute | solution.py:202
  109.6 25.4 %collective-permute-start.3 = (f32[768]{0:T(1024)S(1)}, f32[768]{0:T(1024)S(1)}, u32[]{:S(2)}, u32[]{:S(2)}) collective-permute-start(f32[768]{0:T(1024)S(1)} %reduce.1), channel_id=1, source_target_pairs={{0,6},{1,7},{2,4},{3,5},{4,9},{5,10},{6,11},{7,8},{8,12},{9,13},{1... | collective-permute-start | bytes 9224 | tf_op jit(solution)/shard_map/ppermute | solution.py:202

commit v2 on v1

v2 whole, which is shorter than its diff:
```python
import functools

import jax
import jax.numpy as jnp
from jax import lax
from jax.experimental import pallas as pl
from jax.experimental.pallas import tpu as pltpu
from jax.sharding import PartitionSpec as P

POLAR = 8
STEPS = 2
DEPTH = 256
LANES = 128
CHUNK, ROWS = 256, 32

soft_width = 0.25
floor_term = 0.01

THIRD = (
    0.8660254163908417, 0.16666504306323746, -0.048077350345029135, 0.024392383831939313,
    -0.014289564826206913, 0.007664301754289227, -0.002922830501063345, 0.0005426077123047435,
)


def split3(x):
    one = x.astype(jnp.bfloat16).astype(jnp.float32)
    rest = x - one
    two = rest.astype(jnp.bfloat16).astype(jnp.float32)
    return (one, two, rest - two)


def align_of(h):
    h00, h01, h02, h10, h11, h12, h20, h21, h22 = h
    s00 = h00 * h00 + h10 * h10 + h20 * h20
    s11 = h01 * h01 + h11 * h11 + h21 * h21
    s22 = h02 * h02 + h12 * h12 + h22 * h22
    s01 = h00 * h01 + h10 * h11 + h20 * h21
    s02 = h00 * h02 + h10 * h12 + h20 * h22
    s12 = h01 * h02 + h11 * h12 + h21 * h22
    q02 = s02 * s02
    q12 = s12 * s12
    m01 = s00 * s11 - s01 * s01
    minors = m01 + (s00 * s22 - q02) + (s11 * s22 - q12)
    cross = s01 * s02
    det = s22 * m01 - s11 * q02 - s00 * q12 + (cross + cross) * s12
    trace = s00 + s11 + s22
    size = trace + 1.0
    inverse = lax.rsqrt(size)
    inv2 = inverse * inverse
    third = trace * (1.0 / 3.0)
    third2 = third * third
    p2 = jnp.maximum(third2 - minors * (1.0 / 3.0), 1e-24)
    half = third * (third2 - 0.5 * minors) + 0.5 * det
    ip = lax.rsqrt(p2)
    p = (p2 * ip) * inv2
    r = jnp.minimum(jnp.abs(half * (ip * ip * ip)), 1.0)
    c = THIRD[-1] * r + THIRD[-2]
    for k in THIRD[-3::-1]:
        c = c * r + k
    rest = jnp.maximum(1.0 - c * c, 1e-14)
    wide = (p * 0.8660254037844386) * (rest * lax.rsqrt(rest))
    pc = jnp.where(half < 0.0, -p, p) * c
    middle = third * (0.5 * inv2)
    base = middle - 0.5 * pc
    total = None
    for root in (middle + pc, base + wide, base - wide):
        root = jnp.maximum(root, 1e-20)
        start = root * lax.rsqrt(root)
        v = start * (1.5 - root)
        for _ in range(POLAR - 1):
            v = v * (1.5 - v * v)
        total = start * v if total is None else total + start * v
    return (size * inverse) * total


def near_first(height, width):
    table = []
    for i in range(height):
        first = i % width
        second = ((i + 1) % height + 1) % width
        table.append(int(min(first, width - first) > min(second, width - second)))
    return table


def kernel(height, width, atoms, frames, chunk, rows, thr_ref, gen_ref, ref_ref,
           gbest_ref, rbest_ref, cover_ref, recv, back, ref_t, gen_b, h, rnb, gnb, rmin, rsum, gmin,
           send_sem, recv_sem, bsend_sem, brecv_sem):
    scale = 1.0 / atoms
    unit = 0.25 * atoms
    pieces = frames // chunk
    grp, i, j = lax.axis_index("grp"), lax.axis_index("row"), lax.axis_index("col")
    table = near_first(height, width)

    def slot_of(row):
        slot = jnp.int32(0)
        for k, late in enumerate(table):
            if late:
                slot = slot + jnp.where(row == k, 1, 0)
        return slot

    up, down = lax.rem(i + height - 1, height), lax.rem(i + 1, height)
    wrap = width * (height // width + 2)
    a_to = (grp, i, lax.rem(j + i, width))
    b_to = (grp, up, lax.rem(j + i + 1, width))
    a_from = (grp, i, lax.rem(j + wrap - i, width))
    b_from = (grp, down, lax.rem(j + wrap - down - 1, width))
    at_home = lax.rem(i, width) == 0
    away = lax.rem(i, width) != 0
    a_here = slot_of(i)
    a_slot, b_slot = a_here, 1 - slot_of(up)

    barrier = pltpu.get_barrier_semaphore()
    for other in (b_to, b_from):
        pl.semaphore_signal(barrier, inc=1, device_id=other, device_id_type=pl.DeviceIdType.MESH)

    @pl.when(away)
    def _():
        for other in (a_to, a_from):
            pl.semaphore_signal(barrier, inc=1, device_id=other, device_id_type=pl.DeviceIdType.MESH)

    pl.semaphore_wait(barrier, jnp.where(away, 4, 2))

    def remote(which, k):
        to, slot = ((a_to, a_slot), (b_to, b_slot))[which]
        columns = pl.ds(k * chunk, chunk)
        return pltpu.make_async_remote_copy(
            src_ref=gen_ref.at[:, :, columns], dst_ref=recv.at[slot, :, :, columns],
            send_sem=send_sem.at[which, k], recv_sem=recv_sem.at[slot, k],
            device_id=to, device_id_type=pl.DeviceIdType.MESH)

    def local(k):
        columns = pl.ds(k * chunk, chunk)
        return pltpu.make_async_copy(gen_ref.at[:, :, columns], recv.at[a_slot, :, :, columns],
                                     recv_sem.at[a_slot, k])

    def send(phase):
        @pl.when(jnp.logical_and(a_slot == phase, away))
        def _():
            for k in range(pieces):
                remote(0, k).start()

        @pl.when(jnp.logical_and(a_slot == phase, at_home))
        def _():
            for k in range(pieces):
                local(k).start()

        @pl.when(b_slot == phase)
        def _():
            for k in range(pieces):
                remote(1, k).start()

    send(0)

    def load(x_ref, columns):
        parts = []
        sq = None
        for a in range(3):
            x = x_ref[a, :, columns].astype(jnp.float32)
            total = jnp.sum(x, axis=0, keepdims=True)
            d = x - total * scale
            q = jnp.sum(d * d, axis=0, keepdims=True)
            sq = q if sq is None else sq + q
            parts.append((x, total))
        return parts, sq * (scale * unit)

    def deep(x, values, columns):
        pick = lax.broadcasted_iota(jnp.int32, (16, columns), 0)
        extra = jnp.zeros((16, columns), jnp.float32)
        for k, value in enumerate(values):
            extra = jnp.where(pick == k, value, extra)
        zero = jnp.zeros((DEPTH - atoms - 16, columns), jnp.float32)
        return jnp.concatenate([x, extra, zero], axis=0)

    def prepare(index, carry):
        columns = pl.ds(pl.multiple_of(index * chunk, chunk), chunk)
        parts, sq = load(ref_ref, columns)
        rnb[columns, :] = jnp.broadcast_to(sq + floor_term * unit, (LANES, chunk)).T
        for a, (x, total) in enumerate(parts):
            s = split3(-total)
            ref_t[a, columns, :] = deep(x, [s[k % 3] for k in range(9)], chunk).T.astype(jnp.bfloat16)
        return carry

    lax.fori_loop(0, pieces, prepare, 0)
    rmin[...] = jnp.full(rmin.shape, jnp.inf, jnp.float32)
    rsum[...] = jnp.zeros(rsum.shape, jnp.float32)
    gmin[...] = jnp.full(gmin.shape, jnp.inf, jnp.float32)
    slope = 1.4426950408889634 / soft_width
    limit = thr_ref[0] * slope
    slope = slope * unit ** -0.5

    def piece(slot):
        def run(index, carry):
            columns = pl.ds(pl.multiple_of(index * chunk, chunk), chunk)
            parts, sq = load(recv.at[slot], columns)
            gnb[...] = jnp.broadcast_to(sq, (8, chunk))
            for a, (x, total) in enumerate(parts):
                m = split3(total * scale)
                gen_b[...] = deep(x, [m[k // 3] for k in range(9)], chunk).astype(jnp.bfloat16)
                for b in range(3):
                    h[3 * a + b] = jnp.dot(ref_t[b], gen_b[...], preferred_element_type=jnp.float32)

            def group(step, carry):
                at = pl.ds(pl.multiple_of(step * rows, rows), rows)
                align = align_of([h[k, at, :] for k in range(9)])
                rn = jnp.concatenate([rnb[at, :]] * (chunk // LANES), axis=1)
                gn = jnp.concatenate([gnb[...]] * (rows // 8), axis=0)
                square = rn + gn - align
                rmsd = square * lax.rsqrt(square)
                power = jnp.minimum(rmsd * slope - limit, 120.0)
                below = 1.0 + jnp.exp2(power)
                weight = pl.reciprocal(below, approx=True)
                weight = weight * (2.0 - below * weight)
                low, hits = rmsd[:, :LANES], weight[:, :LANES]
                for k in range(1, chunk // LANES):
                    low = jnp.minimum(low, rmsd[:, k * LANES:(k + 1) * LANES])
                    hits = hits + weight[:, k * LANES:(k + 1) * LANES]
                rmin[at, :] = jnp.minimum(rmin[at, :], low)
                rsum[at, :] = rsum[at, :] + hits
                best = rmsd[:8]
                for k in range(1, rows // 8):
                    best = jnp.minimum(best, rmsd[8 * k:8 * k + 8])
                gmin[slot, :, columns] = jnp.minimum(gmin[slot, :, columns], best)
                return carry

            lax.fori_loop(0, frames // rows, group, 0)
            return carry
        return run

    def arrived(slot, k):
        target = recv.at[slot, :, :, pl.ds(k * chunk, chunk)]
        pltpu.make_async_copy(target, target, recv_sem.at[slot, k]).wait()

    def give_back(slot, which):
        return pltpu.make_async_remote_copy(
            src_ref=gmin.at[slot], dst_ref=back.at[which],
            send_sem=bsend_sem.at[slot], recv_sem=brecv_sem.at[which],
            device_id=(a_from, b_from)[which], device_id_type=pl.DeviceIdType.MESH)

    for slot in range(2):
        for k in range(pieces):
            arrived(slot, k)
            if slot == 0 and k == 0:
                send(1)
            piece(slot)(k, 0)
        here = a_here == slot

        @pl.when(jnp.logical_and(here, away))
        def _():
            give_back(slot, 0).start()

        @pl.when(jnp.logical_and(here, at_home))
        def _():
            pltpu.make_async_copy(gmin.at[slot], back.at[0], brecv_sem.at[0]).start()

        @pl.when(a_here != slot)
        def _():
            give_back(slot, 1).start()

    size = unit ** -0.5
    rbest_ref[...] = jnp.min(rmin[...].T, axis=0, keepdims=True) * size
    cover_ref[...] = jnp.sum(rsum[...].T, axis=0, keepdims=True) * (1.0 / (STEPS * frames))

    for which in range(2):
        pltpu.make_async_copy(back.at[which], back.at[which], brecv_sem.at[which]).wait()
    gbest_ref[...] = jnp.min(jnp.minimum(back[0], back[1]), axis=0, keepdims=True) * size

    @pl.when(away)
    def _():
        for k in range(pieces):
            remote(0, k).wait_send()

    for k in range(pieces):
        remote(1, k).wait_send()
    for slot in range(2):
        @pl.when(jnp.logical_or(away, a_here != slot))
        def _():
            give_back(slot, 0).wait_send()


def on_device(gen_coords, ref_coords, threshold):
    height, width = lax.axis_size("row"), lax.axis_size("col")
    _, atoms, frames = gen_coords.shape
    chunk, rows = min(CHUNK, frames), ROWS
    row = jax.ShapeDtypeStruct((1, frames), jnp.float32)
    vmem = pl.BlockSpec(memory_space=pltpu.VMEM)
    pieces = frames // chunk
    out = pl.pallas_call(
        functools.partial(kernel, height, width, atoms, frames, chunk, rows),
        out_shape=(row, row, row),
        in_specs=[pl.BlockSpec(memory_space=pltpu.SMEM), pl.BlockSpec(memory_space=pl.ANY), vmem],
        out_specs=(vmem, vmem, vmem),
        scratch_shapes=[
            pltpu.VMEM((2, 3, atoms, frames), jnp.bfloat16),
            pltpu.VMEM((2, 8, frames), jnp.float32),
            pltpu.VMEM((3, frames, DEPTH), jnp.bfloat16),
            pltpu.VMEM((DEPTH, chunk), jnp.bfloat16),
            pltpu.VMEM((9, frames, chunk), jnp.float32),
            pltpu.VMEM((frames, LANES), jnp.float32),
            pltpu.VMEM((8, chunk), jnp.float32),
            pltpu.VMEM((frames, LANES), jnp.float32),
            pltpu.VMEM((frames, LANES), jnp.float32),
            pltpu.VMEM((2, 8, frames), jnp.float32),
            pltpu.SemaphoreType.DMA((2, pieces)),
            pltpu.SemaphoreType.DMA((2, pieces)),
            pltpu.SemaphoreType.DMA((2,)),
            pltpu.SemaphoreType.DMA((2,)),
        ],
        compiler_params=pltpu.CompilerParams(
            vmem_limit_bytes=48 * 2**20, collective_id=0, has_side_effects=True),
    )(threshold, gen_coords, ref_coords)
    return tuple(x.reshape(frames) for x in out)


def solution(mesh):
    spread = ("grp", "row", "col")
    return jax.shard_map(
        on_device,
        mesh=mesh,
        in_specs=(P(None, None, spread), P(None, None, spread), P()),
        out_specs=(P(spread), P(spread), P(spread)),
        check_vma=False,
    )
```

time: 136 us -> 71.7 us (0.53)
  the two profiles are of different devices: /device:TPU:1 before, /device:TPU:0 now
where the time goes in v2:
time: 71.7 us; the launch traced here: 71.5 us
  Pallas kernels  66.1 us (92%)
  local copies, waits for them, and re-layouts  2.33 us (3%)
  other arithmetic  1.82 us (3%)
  between operations  1.3 us (2%)
    pallas_call x1, Pallas kernels, on_device(): pl.pallas_call(functools.partial(kernel, height, width, atoms, frames, ch...  66.1 us
    unnamed x4, local copies, waits for them, and re-layouts  2.33 us
    pallas_call x3, other arithmetic, on_device(): pl.pallas_call(functools.partial(kernel, height, width, atoms, frames, ch...  1.82 us

profile of v2, /device:TPU:0, one launch (start us, length us, event | category | flops | bytes accessed | tf_op | source)
XLA Modules:
  0.0 71.5 jit_solution(11517344503112719216)
XLA Ops:
  1.3 0.0 copy-start
  1.3 1.2 %copy-done = bf16[3,192,768]{2,1,0:T(8,128)(2,1)S(1)} copy-done((bf16[3,192,768]{2,1,0:T(8,128)(2,1)S(1)}, bf16[3,192,768]{2,1,0:T(8,128)(2,1)}, u32[]{:S(2)}) %copy-start) | copy-done | bytes 884760
  2.4 0.0 copy-start.1
  2.4 1.2 %copy-done.1 = bf16[3,192,768]{2,1,0:T(8,128)(2,1)S(1)} copy-done((bf16[3,192,768]{2,1,0:T(8,128)(2,1)S(1)}, bf16[3,192,768]{2,1,0:T(8,128)(2,1)}, u32[]{:S(2)}) %copy-start.1) | copy-done | bytes 884760
  3.6 66.1 %shard_map.58 = (f32[1,768]{1,0:T(1,128)S(1)}, f32[1,768]{1,0:T(1,128)S(1)}, f32[1,768]{1,0:T(1,128)S(1)}) custom-call(f32[1]{0:T(128)S(6)} %copy.6.thr_ref, bf16[3,192,768]{2,1,0:T(8,128)(2,1)S(1)} %copy-done, bf16[3,192,768]{2,1,0:T(8,128)(2,1)S(1)} %copy-done.1), custom_call_target="tpu_custom_call" | custom-call | tf_op jit(solution)/shard_map/pallas_call | solution.py:287
  69.7 0.6 reduce
  70.3 0.6 reduce.1
  70.9 0.6 reduce.2
Async XLA Ops:
  1.3 1.2 %copy-start = (bf16[3,192,768]{2,1,0:T(8,128)(2,1)S(1)}, bf16[3,192,768]{2,1,0:T(8,128)(2,1)}, u32[]{:S(2)}) copy-start(bf16[3,192,768]{2,1,0:T(8,128)(2,1)} %gen_ref.1) | copy-start | bytes 2654212
  2.4 1.2 %copy-start.1 = (bf16[3,192,768]{2,1,0:T(8,128)(2,1)S(1)}, bf16[3,192,768]{2,1,0:T(8,128)(2,1)}, u32[]{:S(2)}) copy-start(bf16[3,192,768]{2,1,0:T(8,128)(2,1)} %ref_ref.1) | copy-start | bytes 2654212

commit v3 on v2

--- a/solution.py
+++ b/solution.py
@@ -11,7 +11,7 @@
 STEPS = 2
 DEPTH = 256
 LANES = 128
-CHUNK, ROWS = 256, 32
+CHUNK, ROWS = 256, 64
 
 soft_width = 0.25
 floor_term = 0.01
@@ -82,21 +82,36 @@
     return table
 
 
-def kernel(height, width, atoms, frames, chunk, rows, thr_ref, gen_ref, ref_ref,
-           gbest_ref, rbest_ref, cover_ref, recv, back, ref_t, gen_b, h, rnb, gnb, rmin, rsum, gmin,
-           send_sem, recv_sem, bsend_sem, brecv_sem):
+def handed_on(height, width):
+    late = near_first(height, width)
+    table = []
+    for i in range(height):
+        direct = (i + 1) % width
+        near = min(direct, width - direct) <= 1
+        table.append(int(i % width != 0 and not late[i] and late[i - 1] == 0 and not near))
+    return table
+
+
+def kernel(height, width, atoms, frames, chunk, rows, thr_ref, gen_ref, ref_hbm,
+           gbest_ref, rbest_ref, cover_ref, ref_ref, recv, back, ref_t, gen_b, h, rnb, gnb, rmin, rsum, gmin,
+           send_sem, recv_sem, bsend_sem, brecv_sem, ref_sem):
+    fetch = pltpu.make_async_copy(ref_hbm, ref_ref, ref_sem)
+    fetch.start()
     scale = 1.0 / atoms
     unit = 0.25 * atoms
     pieces = frames // chunk
     grp, i, j = lax.axis_index("grp"), lax.axis_index("row"), lax.axis_index("col")
     table = near_first(height, width)
 
+    def entry(values, row):
+        found = jnp.int32(0)
+        for k, value in enumerate(values):
+            if value:
+                found = found + jnp.where(row == k, 1, 0)
+        return found
+
     def slot_of(row):
-        slot = jnp.int32(0)
-        for k, late in enumerate(table):
-            if late:
-                slot = slot + jnp.where(row == k, 1, 0)
-        return slot
+        return entry(table, row)
 
     up, down = lax.rem(i + height - 1, height), lax.rem(i + 1, height)
     wrap = width * (height // width + 2)
@@ -108,6 +123,11 @@
     away = lax.rem(i, width) != 0
     a_here = slot_of(i)
     a_slot, b_slot = a_here, 1 - slot_of(up)
+    passing = entry(handed_on(height, width), i) == 1
+    keeping = entry(handed_on(height, width), i) == 0
+    next_to = (grp, up, lax.rem(j + 1, width))
+    next_from = (grp, down, lax.rem(j + width - 1, width))
+    sending = entry(handed_on(height, width), down) == 1
 
     barrier = pltpu.get_barrier_semaphore()
     for other in (b_to, b_from):
@@ -118,7 +138,17 @@
         for other in (a_to, a_from):
             pl.semaphore_signal(barrier, inc=1, device_id=other, device_id_type=pl.DeviceIdType.MESH)
 
-    pl.semaphore_wait(barrier, jnp.where(away, 4, 2))
+    @pl.when(passing)
+    def _():
+        pl.semaphore_signal(barrier, inc=1, device_id=next_to, device_id_type=pl.DeviceIdType.MESH)
+
+    @pl.when(sending)
+    def _():
+        pl.semaphore_signal(barrier, inc=1, device_id=next_from, device_id_type=pl.DeviceIdType.MESH)
+
+    pl.semaphore_wait(
+        barrier,
+        2 + jnp.where(away, 2, 0) + jnp.where(passing, 1, 0) + jnp.where(sending, 1, 0))
 
     def remote(which, k):
         to, slot = ((a_to, a_slot), (b_to, b_slot))[which]
@@ -128,6 +158,13 @@
             send_sem=send_sem.at[which, k], recv_sem=recv_sem.at[slot, k],
             device_id=to, device_id_type=pl.DeviceIdType.MESH)
 
+    def onward(k):
+        columns = pl.ds(k * chunk, chunk)
+        return pltpu.make_async_remote_copy(
+            src_ref=recv.at[0, :, :, columns], dst_ref=recv.at[1, :, :, columns],
+            send_sem=send_sem.at[1, k], recv_sem=recv_sem.at[1, k],
+            device_id=next_to, device_id_type=pl.DeviceIdType.MESH)
+
     def local(k):
         columns = pl.ds(k * chunk, chunk)
         return pltpu.make_async_copy(gen_ref.at[:, :, columns], recv.at[a_slot, :, :, columns],
@@ -144,7 +181,7 @@
             for k in range(pieces):
                 local(k).start()
 
-        @pl.when(b_slot == phase)
+        @pl.when(jnp.logical_and(b_slot == phase, keeping))
         def _():
             for k in range(pieces):
                 remote(1, k).start()
@@ -180,6 +217,7 @@
             ref_t[a, columns, :] = deep(x, [s[k % 3] for k in range(9)], chunk).T.astype(jnp.bfloat16)
         return carry
 
+    fetch.wait()
     lax.fori_loop(0, pieces, prepare, 0)
     rmin[...] = jnp.full(rmin.shape, jnp.inf, jnp.float32)
     rsum[...] = jnp.zeros(rsum.shape, jnp.float32)
@@ -241,6 +279,11 @@
             arrived(slot, k)
             if slot == 0 and k == 0:
                 send(1)
+            if slot == 0:
+                @pl.when(passing)
+                def _():
+                    onward(k).start()
+
             piece(slot)(k, 0)
         here = a_here == slot
 
@@ -287,9 +330,10 @@
     out = pl.pallas_call(
         functools.partial(kernel, height, width, atoms, frames, chunk, rows),
         out_shape=(row, row, row),
-        in_specs=[pl.BlockSpec(memory_space=pltpu.SMEM), pl.BlockSpec(memory_space=pl.ANY), vmem],
+        in_specs=[pl.BlockSpec(memory_space=pltpu.SMEM)] + [pl.BlockSpec(memory_space=pltpu.HBM)] * 2,
         out_specs=(vmem, vmem, vmem),
         scratch_shapes=[
+            pltpu.VMEM((3, atoms, frames), jnp.bfloat16),
             pltpu.VMEM((2, 3, atoms, frames), jnp.bfloat16),
             pltpu.VMEM((2, 8, frames), jnp.float32),
             pltpu.VMEM((3, frames, DEPTH), jnp.bfloat16),
@@ -304,6 +348,7 @@
             pltpu.SemaphoreType.DMA((2, pieces)),
             pltpu.SemaphoreType.DMA((2,)),
             pltpu.SemaphoreType.DMA((2,)),
+            pltpu.SemaphoreType.DMA,
         ],
         compiler_params=pltpu.CompilerParams(
             vmem_limit_bytes=48 * 2**20, collective_id=0, has_side_effects=True),

time: 71.7 us -> 68.9 us (0.961)
  Pallas kernels: 66.1 us -> 63.2 us
    pallas_call x1, Pallas kernels: 66.1 us -> 63.2 us  [on_device(): pl.pallas_call(functools.partial(kernel, height, width, atoms, frames, ch...]
where the time goes in v3:
time: 68.9 us; the launch traced here: 68.7 us
  Pallas kernels  63.2 us (92%)
  local copies, waits for them, and re-layouts  2.33 us (3%)
  other arithmetic  1.82 us (3%)
  between operations  1.3 us (2%)
    pallas_call x1, Pallas kernels, on_device(): pl.pallas_call(functools.partial(kernel, height, width, atoms, frames, ch...  63.2 us
    unnamed x4, local copies, waits for them, and re-layouts  2.33 us
    pallas_call x3, other arithmetic, on_device(): pl.pallas_call(functools.partial(kernel, height, width, atoms, frames, ch...  1.82 us

profile of v3, /device:TPU:0, one launch (start us, length us, event | category | flops | bytes accessed | tf_op | source)
XLA Modules:
  0.0 68.7 jit_solution(14144819263912391781)
XLA Ops:
  1.3 0.0 copy-start
  1.3 1.2 %copy-done = bf16[3,192,768]{2,1,0:T(8,128)(2,1)S(1)} copy-done((bf16[3,192,768]{2,1,0:T(8,128)(2,1)S(1)}, bf16[3,192,768]{2,1,0:T(8,128)(2,1)}, u32[]{:S(2)}) %copy-start) | copy-done | bytes 884760
  2.4 0.0 copy-start.1
  2.4 1.2 %copy-done.1 = bf16[3,192,768]{2,1,0:T(8,128)(2,1)S(1)} copy-done((bf16[3,192,768]{2,1,0:T(8,128)(2,1)S(1)}, bf16[3,192,768]{2,1,0:T(8,128)(2,1)}, u32[]{:S(2)}) %copy-start.1) | copy-done | bytes 884760
  3.6 63.2 %shard_map.58 = (f32[1,768]{1,0:T(1,128)S(1)}, f32[1,768]{1,0:T(1,128)S(1)}, f32[1,768]{1,0:T(1,128)S(1)}) custom-call(f32[1]{0:T(128)S(6)} %copy.6.thr_ref, bf16[3,192,768]{2,1,0:T(8,128)(2,1)S(1)} %copy-done, bf16[3,192,768]{2,1,0:T(8,128)(2,1)S(1)} %copy-done.1), custom_call_target="tpu_custom_call" | custom-call | tf_op jit(solution)/shard_map/pallas_call | solution.py:330
  66.8 0.6 reduce
  67.4 0.6 reduce.1
  68.1 0.6 reduce.2
Async XLA Ops:
  1.3 1.2 %copy-start = (bf16[3,192,768]{2,1,0:T(8,128)(2,1)S(1)}, bf16[3,192,768]{2,1,0:T(8,128)(2,1)}, u32[]{:S(2)}) copy-start(bf16[3,192,768]{2,1,0:T(8,128)(2,1)} %gen_ref.1) | copy-start | bytes 2654212
  2.4 1.2 %copy-start.1 = (bf16[3,192,768]{2,1,0:T(8,128)(2,1)S(1)}, bf16[3,192,768]{2,1,0:T(8,128)(2,1)}, u32[]{:S(2)}) copy-start(bf16[3,192,768]{2,1,0:T(8,128)(2,1)} %ref_hbm.1) | copy-start | bytes 2654212

commit v4 on v3

--- a/solution.py
+++ b/solution.py
@@ -123,11 +123,12 @@
     away = lax.rem(i, width) != 0
     a_here = slot_of(i)
     a_slot, b_slot = a_here, 1 - slot_of(up)
-    passing = entry(handed_on(height, width), i) == 1
-    keeping = entry(handed_on(height, width), i) == 0
+    passes = entry(handed_on(height, width), i)
+    passing = jnp.logical_and(passes == 1, j != width - 1)
+    keeping = jnp.logical_or(passes == 0, lax.rem(j + i, width) == width - 1)
     next_to = (grp, up, lax.rem(j + 1, width))
     next_from = (grp, down, lax.rem(j + width - 1, width))
-    sending = entry(handed_on(height, width), down) == 1
+    sending = jnp.logical_and(entry(handed_on(height, width), down) == 1, j != 0)
 
     barrier = pltpu.get_barrier_semaphore()
     for other in (b_to, b_from):
@@ -162,7 +163,7 @@
         columns = pl.ds(k * chunk, chunk)
         return pltpu.make_async_remote_copy(
             src_ref=recv.at[0, :, :, columns], dst_ref=recv.at[1, :, :, columns],
-            send_sem=send_sem.at[1, k], recv_sem=recv_sem.at[1, k],
+            send_sem=send_sem.at[2, k], recv_sem=recv_sem.at[1, k],
             device_id=next_to, device_id_type=pl.DeviceIdType.MESH)
 
     def local(k):
@@ -312,8 +313,16 @@
         for k in range(pieces):
             remote(0, k).wait_send()
 
-    for k in range(pieces):
-        remote(1, k).wait_send()
+    @pl.when(keeping)
+    def _():
+        for k in range(pieces):
+            remote(1, k).wait_send()
+
+    @pl.when(passing)
+    def _():
+        for k in range(pieces):
+            onward(k).wait_send()
+
     for slot in range(2):
         @pl.when(jnp.logical_or(away, a_here != slot))
         def _():
@@ -344,7 +353,7 @@
             pltpu.VMEM((frames, LANES), jnp.float32),
             pltpu.VMEM((frames, LANES), jnp.float32),
             pltpu.VMEM((2, 8, frames), jnp.float32),
-            pltpu.SemaphoreType.DMA((2, pieces)),
+            pltpu.SemaphoreType.DMA((3, pieces)),
             pltpu.SemaphoreType.DMA((2, pieces)),
             pltpu.SemaphoreType.DMA((2,)),
             pltpu.SemaphoreType.DMA((2,)),

time: 68.9 us -> 68.9 us (level)
  no operation moved by 1% of the time
where the time goes in v4:
time: 68.9 us; the launch traced here: 68.7 us
  Pallas kernels  63.2 us (92%)
  local copies, waits for them, and re-layouts  2.33 us (3%)
  other arithmetic  1.82 us (3%)
  between operations  1.3 us (2%)
    pallas_call x1, Pallas kernels, on_device(): pl.pallas_call(functools.partial(kernel, height, width, atoms, frames, ch...  63.2 us
    unnamed x4, local copies, waits for them, and re-layouts  2.33 us
    pallas_call x3, other arithmetic, on_device(): pl.pallas_call(functools.partial(kernel, height, width, atoms, frames, ch...  1.82 us

profile of v4, /device:TPU:0, one launch (start us, length us, event | category | flops | bytes accessed | tf_op | source)
XLA Modules:
  0.0 68.7 jit_solution(11637274798767036310)
XLA Ops:
  1.3 0.0 copy-start
  1.3 1.2 %copy-done = bf16[3,192,768]{2,1,0:T(8,128)(2,1)S(1)} copy-done((bf16[3,192,768]{2,1,0:T(8,128)(2,1)S(1)}, bf16[3,192,768]{2,1,0:T(8,128)(2,1)}, u32[]{:S(2)}) %copy-start) | copy-done | bytes 884760
  2.4 0.0 copy-start.1
  2.4 1.2 %copy-done.1 = bf16[3,192,768]{2,1,0:T(8,128)(2,1)S(1)} copy-done((bf16[3,192,768]{2,1,0:T(8,128)(2,1)S(1)}, bf16[3,192,768]{2,1,0:T(8,128)(2,1)}, u32[]{:S(2)}) %copy-start.1) | copy-done | bytes 884760
  3.6 63.2 %shard_map.58 = (f32[1,768]{1,0:T(1,128)S(1)}, f32[1,768]{1,0:T(1,128)S(1)}, f32[1,768]{1,0:T(1,128)S(1)}) custom-call(f32[1]{0:T(128)S(6)} %copy.6.thr_ref, bf16[3,192,768]{2,1,0:T(8,128)(2,1)S(1)} %copy-done, bf16[3,192,768]{2,1,0:T(8,128)(2,1)S(1)} %copy-done.1), custom_call_target="tpu_custom_call" | custom-call | tf_op jit(solution)/shard_map/pallas_call | solution.py:339
  66.9 0.6 reduce
  67.5 0.6 reduce.1
  68.1 0.6 reduce.2
Async XLA Ops:
  1.3 1.2 %copy-start = (bf16[3,192,768]{2,1,0:T(8,128)(2,1)S(1)}, bf16[3,192,768]{2,1,0:T(8,128)(2,1)}, u32[]{:S(2)}) copy-start(bf16[3,192,768]{2,1,0:T(8,128)(2,1)} %gen_ref.1) | copy-start | bytes 2654212
  2.4 1.2 %copy-start.1 = (bf16[3,192,768]{2,1,0:T(8,128)(2,1)S(1)}, bf16[3,192,768]{2,1,0:T(8,128)(2,1)}, u32[]{:S(2)}) copy-start(bf16[3,192,768]{2,1,0:T(8,128)(2,1)} %ref_hbm.1) | copy-start | bytes 2654212

commit v5 on v4

--- a/solution.py
+++ b/solution.py
@@ -218,6 +218,7 @@
             ref_t[a, columns, :] = deep(x, [s[k % 3] for k in range(9)], chunk).T.astype(jnp.bfloat16)
         return carry
 
+    send(1)
     fetch.wait()
     lax.fori_loop(0, pieces, prepare, 0)
     rmin[...] = jnp.full(rmin.shape, jnp.inf, jnp.float32)
@@ -278,8 +279,6 @@
     for slot in range(2):
         for k in range(pieces):
             arrived(slot, k)
-            if slot == 0 and k == 0:
-                send(1)
             if slot == 0:
                 @pl.when(passing)
                 def _():

time: 68.9 us -> 70.7 us (1.026)
  Pallas kernels: 63.2 us -> 65.1 us
    pallas_call x1, Pallas kernels: 63.2 us -> 65.1 us  [on_device(): pl.pallas_call(functools.partial(kernel, height, width, atoms, frames, ch...]
where the time goes in v5:
time: 70.7 us; the launch traced here: 70.5 us
  Pallas kernels  65.1 us (92%)
  local copies, waits for them, and re-layouts  2.33 us (3%)
  other arithmetic  1.82 us (3%)
  between operations  1.3 us (2%)
    pallas_call x1, Pallas kernels, on_device(): pl.pallas_call(functools.partial(kernel, height, width, atoms, frames, ch...  65.1 us
    unnamed x4, local copies, waits for them, and re-layouts  2.33 us
    pallas_call x3, other arithmetic, on_device(): pl.pallas_call(functools.partial(kernel, height, width, atoms, frames, ch...  1.82 us

profile of v5, /device:TPU:0, one launch (start us, length us, event | category | flops | bytes accessed | tf_op | source)
XLA Modules:
  0.0 70.5 jit_solution(474908089866616513)
XLA Ops:
  1.3 0.0 copy-start
  1.3 1.2 %copy-done = bf16[3,192,768]{2,1,0:T(8,128)(2,1)S(1)} copy-done((bf16[3,192,768]{2,1,0:T(8,128)(2,1)S(1)}, bf16[3,192,768]{2,1,0:T(8,128)(2,1)}, u32[]{:S(2)}) %copy-start) | copy-done | bytes 884760
  2.4 0.0 copy-start.1
  2.4 1.2 %copy-done.1 = bf16[3,192,768]{2,1,0:T(8,128)(2,1)S(1)} copy-done((bf16[3,192,768]{2,1,0:T(8,128)(2,1)S(1)}, bf16[3,192,768]{2,1,0:T(8,128)(2,1)}, u32[]{:S(2)}) %copy-start.1) | copy-done | bytes 884760
  3.6 65.1 %shard_map.58 = (f32[1,768]{1,0:T(1,128)S(1)}, f32[1,768]{1,0:T(1,128)S(1)}, f32[1,768]{1,0:T(1,128)S(1)}) custom-call(f32[1]{0:T(128)S(6)} %copy.6.thr_ref, bf16[3,192,768]{2,1,0:T(8,128)(2,1)S(1)} %copy-done, bf16[3,192,768]{2,1,0:T(8,128)(2,1)S(1)} %copy-done.1), custom_call_target="tpu_custom_call" | custom-call | tf_op jit(solution)/shard_map/pallas_call | solution.py:338
  68.7 0.6 reduce
  69.3 0.6 reduce.1
  69.9 0.6 reduce.2
Async XLA Ops:
  1.3 1.2 %copy-start = (bf16[3,192,768]{2,1,0:T(8,128)(2,1)S(1)}, bf16[3,192,768]{2,1,0:T(8,128)(2,1)}, u32[]{:S(2)}) copy-start(bf16[3,192,768]{2,1,0:T(8,128)(2,1)} %gen_ref.1) | copy-start | bytes 2654212
  2.4 1.2 %copy-start.1 = (bf16[3,192,768]{2,1,0:T(8,128)(2,1)S(1)}, bf16[3,192,768]{2,1,0:T(8,128)(2,1)}, u32[]{:S(2)}) copy-start(bf16[3,192,768]{2,1,0:T(8,128)(2,1)} %ref_hbm.1) | copy-start | bytes 2654212
